TPU v7x, 512 devices: a whole 4x4x16 slice. The times are simulated.
512 devices in a mesh: req: 32 (over x, y, core), head: 16 (over z).
Axes of the slice: x: 4, y: 4, z: 16, core: 2. Of those that a mesh axis runs over, the one named last changes fastest.
Arguments:
- queries: bfloat16 [384, 64, 4096], P('req', None, 'head'), may hold values from -1.796875 to 1.796875
- key_rows: bfloat16 [384, 64, 4096], P('req', None, 'head'), may hold values from -1.796875 to 1.796875
- values: bfloat16 [384, 64, 4096], P('req', None, 'head'), may hold values from -64 to 64
- log_decay: float32 [384, 32, 64], P('req', 'head'), may hold values from -1 to 0
- state_cache: float32 [384, 32, 128, 128], P('req', 'head'), may hold values from -24 to 24
- norm_gain: float32 [4096], P('head'), may hold values from 0.1 to 1.9
- entry_slot: int32 [384], replicated, may hold values from 0 to 383, as said below
- hit_entry: int32 [384], P('req'), may hold values from -1 to 383, as said below
- write_entry: int32 [384], P('req'), may hold values from -1 to 383, as said below
Outputs:
- attended: bfloat16 [384, 64, 4096], P('req', None, 'head')
- new_cache: float32 [384, 32, 128, 128], P('req', 'head')
Inputs may be any that keep to these rules, and one draw needn't show every extreme that they name: `entry_slot`: a permutation. `hit_entry`: slot s is held by index s // 12 of req; the entries named by the 12 requests of one index of req lie on different indices. `write_entry`: no entry is named twice; the entries named by the 12 requests of one index of req lie on different indices.
All inputs are finite; a program needn't handle non-finite values.
Results may differ from a plain program's by a relative error of at most 0.0048.
Values sent between devices are 32-bit elements; how exact they have to be, the bound alone decides.
A program may use at most 128 MiB of HBM per device.

v0:
```python
import jax
import jax.numpy as jnp
from jax import lax
from jax.sharding import PartitionSpec as P


def block_terms(operands):
    query_rows, key_block, value_block, gsum = operands
    length = query_rows.shape[0]
    head_count = gsum.shape[0]
    head_size = query_rows.shape[1] // head_count
    query_heads = query_rows.reshape(length, head_count, head_size)
    key_heads = key_block.reshape(length, head_count, head_size)
    value_heads = value_block.reshape(length, head_count, head_size)
    scores = jnp.einsum("thd,shd->hts", query_heads, key_heads, preferred_element_type=jnp.float32)
    gap_sums = gsum[:, :, None] - gsum[:, None, :]
    causal = lax.broadcasted_iota(jnp.int32, (length, length), 0) >= lax.broadcasted_iota(
        jnp.int32, (length, length), 1
    )
    weights = (scores * jnp.where(causal, jnp.exp(jnp.minimum(gap_sums, 0.0)), 0.0)).astype(
        jnp.bfloat16
    )
    local_part = jnp.einsum(
        "hts,shd->thd", weights, value_heads, preferred_element_type=jnp.float32
    )
    tail_decay = jnp.exp(gsum[:, -1:] - gsum).T
    weighted_keys = (key_heads.astype(jnp.float32) * tail_decay[:, :, None]).astype(jnp.bfloat16)
    carried_keys = jnp.einsum(
        "shi,shj->hij", weighted_keys, value_heads, preferred_element_type=jnp.float32
    )
    return (local_part, carried_keys)


def body(
    queries, key_rows, values, log_decay, state_cache, norm_gain, entry_slot, hit_entry, write_entry
):
    req_count, length, feature_width = queries.shape
    head_count = log_decay.shape[1]
    head_size = state_cache.shape[2]
    entry_count = state_cache.shape[0]
    device_count = lax.axis_size("req")
    device_row = lax.axis_index("req")
    gsum = jnp.cumsum(log_decay, axis=2)
    hit_slot = jnp.where(hit_entry >= 0, entry_slot[jnp.maximum(hit_entry, 0)], -1)
    write_slot = jnp.where(write_entry >= 0, entry_slot[jnp.maximum(write_entry, 0)], -1)
    all_hits, all_writes = (
        lax.all_gather(hit_slot, "req", axis=0, tiled=True),
        lax.all_gather(write_slot, "req", axis=0, tiled=True),
    )
    first_own = device_row * entry_count
    local_part, carried_keys = lax.map(block_terms, (queries, key_rows, values, gsum))
    hit_mask = hit_slot >= 0
    empty = jnp.zeros((req_count, head_count, head_size, head_size), jnp.float32)
    shard_rows = lax.all_gather(state_cache, "req", axis=0, tiled=True)
    inside = hit_mask & (hit_slot >= 0) & (hit_slot < shard_rows.shape[0])
    clipped = jnp.clip(hit_slot, 0, shard_rows.shape[0] - 1)
    prefix = jnp.where(inside[:, None, None, None], jnp.take(shard_rows, clipped, axis=0), empty)
    prefix_high = prefix.astype(jnp.bfloat16)
    prefix_low = (prefix - lax.optimization_barrier(prefix_high).astype(jnp.float32)).astype(
        jnp.bfloat16
    )
    query_heads = queries.reshape(req_count, length, head_count, head_size)
    decay_now = jnp.exp(gsum).transpose(0, 2, 1)[:, :, :, None]
    carried = jnp.einsum(
        "rthi,rhij->rthj", query_heads, prefix_high, preferred_element_type=jnp.float32
    )
    carried = carried + jnp.einsum(
        "rthi,rhij->rthj", query_heads, prefix_low, preferred_element_type=jnp.float32
    )
    heads_out = (local_part + carried * decay_now).reshape(req_count, length, feature_width)
    square_total = lax.psum(jnp.sum(heads_out * heads_out, axis=2), "head")
    inv_rms = lax.rsqrt(square_total / (feature_width * lax.axis_size("head")) + 1e-06)
    attended = (heads_out * inv_rms[:, :, None] * norm_gain).astype(jnp.bfloat16)
    final_state = jnp.exp(gsum[:, :, -1])[:, :, None, None] * prefix + carried_keys
    target_holder = jnp.where(write_slot >= 0, write_slot // entry_count, -1)
    sending = jnp.arange(device_count, dtype=jnp.int32)[:, None] == target_holder[None, :]
    send_pick = jnp.sum(
        jnp.where(sending, jnp.arange(req_count, dtype=jnp.int32)[None, :], 0), axis=1
    )
    send_flag = jnp.any(sending, axis=1)
    outgoing_back = jnp.where(
        send_flag[:, None, None, None], jnp.take(final_state, send_pick, axis=0), 0.0
    )
    returned = lax.all_to_all(outgoing_back, "req", split_axis=0, concat_axis=0, tiled=True)
    peer_writes = all_writes.reshape(device_count, req_count)
    write_local = peer_writes - first_own
    write_match = (peer_writes >= 0)[:, :, None] & (
        write_local[:, :, None] == jnp.arange(entry_count, dtype=jnp.int32)[None, None, :]
    )
    source_row = jnp.sum(
        jnp.where(write_match, jnp.arange(device_count, dtype=jnp.int32)[:, None, None], 0),
        axis=(0, 1),
    )
    written = jnp.any(write_match, axis=(0, 1))
    new_cache = jnp.where(
        written[:, None, None, None], jnp.take(returned, source_row, axis=0), state_cache
    )
    return (attended, new_cache)


def solution(mesh):
    placed = (
        P("req", None, "head"),
        P("req", None, "head"),
        P("req", None, "head"),
        P("req", "head", None),
        P("req", "head", None, None),
        P("head"),
        P(),
        P("req"),
        P("req"),
    )
    return jax.shard_map(
        body,
        mesh=mesh,
        in_specs=placed,
        out_specs=(P("req", None, "head"), P("req", "head", None, None)),
        check_vma=False,
    )
```

profile of v0, /device:TPU:4, one launch (start us, length us, event | category | flops | bytes accessed | tf_op | source)
XLA Modules:
  0.0 311.4 jit_solution(2871083170944259602)
XLA Ops:
  7.3 0.7 all-gather.2.cloned.1.call-update
  10.1 1.3 dynamic-slice
  14.7 46.4 %while.13 = (s32[]{:T(128)}, f32[12,64,2,128]{3,1,2,0:T(8,128)}, f32[12,2,128,128]{3,2,1,0:T(8,128)}, bf16[12,64,256]{2,1,0:T(8,128)(2,1)}, bf16[12,64,256]{2,1,...) while((s32[]{:T(128)}, f32[12,64,2,128]{3,1,2,0:T(8,128)}, ...), condition=%wide.region_2.3_spmd.clone, body=%wide.region_1.2_spmd.sunk.clone | while | flops 8482946 | bytes 838257 | solution.py:51
  15.0 0.8 constant_dynamic-slice_fusion.10
  16.0 0.8 constant_dynamic-slice_fusion.12
  16.8 0.9 fusion.66
  17.7 0.9 fusion.65
  18.9 0.8 constant_dynamic-slice_fusion.10
  19.8 0.8 constant_dynamic-slice_fusion.12
  20.6 0.9 fusion.66
  21.5 0.9 fusion.65
  22.8 0.8 constant_dynamic-slice_fusion.10
  23.7 0.8 constant_dynamic-slice_fusion.12
  24.5 0.9 fusion.66
  25.4 0.9 fusion.65
  26.6 0.8 constant_dynamic-slice_fusion.10
  27.6 0.8 constant_dynamic-slice_fusion.12
  28.4 0.9 fusion.66
  29.3 0.9 fusion.65
  30.5 0.8 constant_dynamic-slice_fusion.10
  31.4 0.8 constant_dynamic-slice_fusion.12
  32.2 0.9 fusion.66
  33.1 0.9 fusion.65
  34.4 0.8 constant_dynamic-slice_fusion.10
  35.3 0.8 constant_dynamic-slice_fusion.12
  36.1 0.9 fusion.66
  37.0 0.9 fusion.65
  38.2 0.8 constant_dynamic-slice_fusion.10
  39.2 0.8 constant_dynamic-slice_fusion.12
  40.0 0.9 fusion.66
  40.9 0.9 fusion.65
  42.1 0.8 constant_dynamic-slice_fusion.10
  43.0 0.8 constant_dynamic-slice_fusion.12
  43.8 0.9 fusion.66
  44.7 0.9 fusion.65
  46.0 0.8 constant_dynamic-slice_fusion.10
  46.9 0.8 constant_dynamic-slice_fusion.12
  47.7 0.9 fusion.66
  48.6 0.9 fusion.65
  49.9 0.8 constant_dynamic-slice_fusion.10
  50.8 0.8 constant_dynamic-slice_fusion.12
  51.6 0.9 fusion.66
  52.5 0.9 fusion.65
  53.7 0.8 constant_dynamic-slice_fusion.10
  54.6 0.8 constant_dynamic-slice_fusion.12
  55.4 0.9 fusion.66
  56.3 0.9 fusion.65
  57.6 0.8 constant_dynamic-slice_fusion.10
  58.5 0.8 constant_dynamic-slice_fusion.12
  59.3 0.9 fusion.66
  60.2 0.9 fusion.65
  61.7 126.8 %all-gather.2.cloned.1.call-done = f32[384,2,128,128]{3,2,1,0:T(8,128)} async-done(((f32[12,2,128,128]{3,2,1,0:T(8,128)}), f32[384,2,128,128]{3,2,1,0:T(8,128)}) %all-gather.2.cloned.1.call-update) | async-done | bytes 50331664 | tf_op jit(solution)/shard_map/all_gather | solution.py:54
  188.5 2.1 gather_fusion.1
  190.6 1.7 multiply_add_fusion
  192.3 2.9 gather_fusion.3
  195.2 5.1 %select_select_fusion = f32[32,2,128,128]{3,2,1,0:T(8,128)} fusion(f32[32,2,128,128]{3,2,1,0:T(8,128)} %gather_fusion.3, pred[32]{0:T(512)(128)(4,1)S(1)} %copy-done.13, pred[32]{0:T(512)(128)(4,1)S(1)} %copy-done.12), kind=kLoop, calls=%fused_computation.33 | loop fusion | flops 2097152 | bytes 8388672 | tf_op jit(solution)/shard_map/jit(_where)/select_n | solution.py:81
  200.3 5.5 %all-to-all-start = ((f32[32,2,128,128]{3,2,1,0:T(8,128)}), f32[32,2,128,128]{3,2,1,0:T(8,128)}, u32[]{:S(2)}, u32[]{:S(2)}) async-start(f32[32,2,128,128]{3,2,1,0:T(8,128)} %select_select_fusion), calls=%async_computation | async-start | bytes 8388608 | tf_op jit(solution)/shard_map/all_to_all | solution.py:84
  205.9 58.3 %all-reduce = s32[384]{0:T(512)S(1)} all-reduce(s32[384]{0:T(512)S(1)} %get-tuple-element.95), channel_id=1, replica_groups=mesh['req'=32,'head'=16] {'req'}, use_global_device_ids=true, to_apply=%add | all-reduce | flops 384 | bytes 3072
  265.6 0.8 copy-done.4
  266.4 0.9 multiply_reduce_fusion
  267.3 31.8 %psum.7 = f32[12,64]{1,0:T(8,128)S(1)} all-reduce(f32[12,64]{1,0:T(8,128)S(1)} %get-tuple-element.98), channel_id=1, replica_groups=mesh['req'=32,'head'=16] {'head'}, use_global_device_ids=true, to_apply=%region_4.5 | all-reduce | flops 768 | bytes 6144 | tf_op jit(solution)/shard_map/psum | solution.py:71
  299.2 0.9 fusion.24
  300.1 3.0 gather_fusion.4
  303.1 1.5 select_select_fusion.1
  (178 shorter events, 13.5 us)
Async XLA Ops:
  7.2 1.6 copy-start
  7.2 0.8 copy-start.7
  7.2 1.6 copy-start.14
  7.2 2.2 copy-start.15
  7.2 7.5 %copy-start.3 = (bf16[12,64,256]{2,1,0:T(8,128)(2,1)S(1)}, bf16[12,64,256]{2,1,0:T(8,128)(2,1)}, u32[]{:S(2)}) copy-start(bf16[12,64,256]{2,1,0:T(8,128)(2,1)} %param.11) | copy-start | bytes 1179652
  7.2 181.2 %all-gather.2.cloned.1.call-start = ((), (), s32[]{:S(2)}) async-start(), calls=%async_computation.1 | async-start | bytes 51904512 | tf_op jit(solution)/shard_map/all_gather | solution.py:54
  61.1 0.6 copy-start.5
  61.7 128.8 %copy-start.8 = (pred[12]{0:T(512)(128)(4,1)S(1)}, pred[12]{0:T(512)(128)(4,1)}, u32[]{:S(2)}) copy-start(pred[12]{0:T(512)(128)(4,1)} %get-tuple-element.91) | copy-start | bytes 40
  192.3 2.9 copy-start.12
  192.3 2.9 copy-start.13
  200.3 5.6 %copy-start.6 = (f32[12,2,64]{2,0,1:T(8,128)S(1)}, f32[12,2,64]{2,0,1:T(8,128)}, u32[]{:S(2)}) copy-start(f32[12,2,64]{2,0,1:T(8,128)} %copy-done.5) | copy-start | bytes 18436
  200.3 64.6 %copy-start.9 = (pred[12]{0:T(512)(128)(4,1)S(1)}, pred[12]{0:T(512)(128)(4,1)}, u32[]{:S(2)}) copy-start(pred[12]{0:T(512)(128)(4,1)} %get-tuple-element.91) | copy-start | bytes 40
  200.3 64.6 %copy-start.10 = (pred[12]{0:T(512)(128)(4,1)S(1)}, pred[12]{0:T(512)(128)(4,1)}, u32[]{:S(2)}) copy-start(pred[12]{0:T(512)(128)(4,1)} %get-tuple-element.97) | copy-start | bytes 40
  200.3 99.8 %all-to-all-start = ((f32[32,2,128,128]{3,2,1,0:T(8,128)}), f32[32,2,128,128]{3,2,1,0:T(8,128)}, u32[]{:S(2)}, u32[]{:S(2)}) async-start(f32[32,2,128,128]{3,2,1,0:T(8,128)} %select_select_fusion), calls=%async_computation | async-start | bytes 8388608 | tf_op jit(solution)/shard_map/all_to_all | solution.py:84
  265.3 1.1 copy-start.4
  266.4 32.8 %copy-start.11 = (f32[256]{0:T(256)S(1)}, f32[256]{0:T(256)}, u32[]{:S(2)}) copy-start(f32[256]{0:T(256)} %param.16) | copy-start | bytes 3076
  300.1 3.0 copy-start.2
  300.1 4.4 %copy-start.1 = (s32[384]{0:T(512)S(1)}, s32[384]{0:T(512)}, u32[]{:S(2)}) copy-start(s32[384]{0:T(512)} %param.17) | copy-start | bytes 4612
Sparse Core Ops, SparseCore 0:
  11.2 177.2 all-gather.1
where the time goes:
time: 314 us; the launch traced here: 311 us
  waiting for transfers between devices  127 us (40%)
  blocking collectives  90.1 us (29%)
  local copies, waits for them, and re-layouts  35.2 us (11%)
  matrix products  22.3 us (7%)
  other arithmetic  15.5 us (5%)
  between operations  14.9 us (5%)
  starting transfers between devices  5.58 us (2%)
    all_gather x1, waiting for transfers between devices, body(): shard_rows = lax.all_gather(state_cache, 'req', axis=0, tiled=True)  127 us
    unnamed x1, blocking collectives  58.3 us
    psum x1, blocking collectives, body(): square_total = lax.psum(jnp.sum(heads_out * heads_out, axis=2), 'head')  31.8 us
    dynamic_slice x36, local copies, waits for them, and re-layouts, body(): lax.map(block_terms, (queries, key_rows, values, gsum))  18.5 us
    dot_general x12, matrix products, block_terms(): jnp.einsum('shi,shj->hij', weighted_keys, value_heads, preferred_element_...  10.5 us
    dot_general x12, matrix products, block_terms(): jnp.einsum('hts,shd->thd', weights, value_heads, preferred_element_type=j...  10.5 us
  transfers between devices with their start and end apart: 2, of which 1 were waited for; matrix products, arithmetic and copies ran while one was open for 18% of the time, Pallas kernels for 0%

commit v1 on v0

v1 whole, which is shorter than its diff:
```python
import functools

import jax
import jax.numpy as jnp
from jax import lax
from jax.experimental import pallas as pl
from jax.experimental.pallas import tpu as pltpu
from jax.sharding import PartitionSpec as P

MESH = pl.DeviceIdType.MESH
F32 = jnp.float32
BF16 = jnp.bfloat16
LANES = 128
HIT, WRITE = 0, 16


def nt(a, b, **kw):
    return lax.dot_general(a, b, (((1,), (1,)), ((), ())), preferred_element_type=F32, **kw)


def tn(a, b):
    return lax.dot_general(a, b, (((0,), (0,)), ((), ())), preferred_element_type=F32)


def kernel(
    n, nz, entry_slot, hit_entry, write_entry, log_decay, queries, key_rows, values, gain, cache,
    attended, new_cache,
    pieces, kv_pieces, kv, hit_pieces, new_pieces, prefix, heads, decay_cols, own_slots, slots,
    own_decay, decays, inverse, own_squares, squares, slots_s, decays_s, inverse_s,
    slot_send, slot_recv, decay_send, decay_recv, cache_send, cache_recv, kv_send, kv_recv,
    hit_send, hit_recv, new_send, new_recv, square_send, square_recv, local_sem,
):
    count, length, width = queries.shape
    head_count = log_decay.shape[1]
    size = width // head_count
    rows = cache.shape[1] // n
    me, z = lax.axis_index("req"), lax.axis_index("head")

    def peer_of(d):
        x, y, c = me // 8, (me // 2) % 4, me % 2
        return ((x + d // 8) % 4) * 8 + ((y + (d // 2) % 4) % 4) * 2 + (c + d % 2) % 2

    def each_peer(act):
        def step(d, carry):
            act(d, peer_of(d))
            return carry

        lax.fori_loop(1, n, step, 0)

    def each_z(act):
        def step(d, carry):
            act(d, lax.rem(z + d, nz))
            return carry

        lax.fori_loop(1, nz, step, 0)

    def remote(src, dst, send, recv, device):
        return pltpu.make_async_remote_copy(
            src_ref=src, dst_ref=dst, send_sem=send, recv_sem=recv, device_id=device, device_id_type=MESH
        )

    def part(ref, device):
        return ref.at[pl.ds(device * count, count)]

    def strip(ref, device):
        return ref.at[:, pl.ds(pl.multiple_of(device * rows, rows), rows), :]

    def slot_copy(d, peer):
        return remote(own_slots, slots.at[me], slot_send.at[d], slot_recv.at[d], (peer, z))

    def decay_copy(d, peer):
        return remote(own_decay, decays.at[me], decay_send.at[d], decay_recv.at[d], (peer, z))

    def cache_copy(d, peer):
        return remote(strip(cache, peer), part(pieces, me), cache_send.at[d], cache_recv.at[d], (peer, z))

    def kv_copy(d, peer):
        return remote(strip(kv, peer), part(kv_pieces, me), kv_send.at[d], kv_recv.at[d], (peer, z))

    def hit_copy(d, peer):
        return remote(part(hit_pieces, peer), strip(prefix, me), hit_send.at[d], hit_recv.at[d], (peer, z))

    def new_copy(d, peer):
        return remote(part(new_pieces, peer), strip(new_cache, me), new_send.at[d], new_recv.at[d], (peer, z))

    def square_copy(d, peer):
        return remote(own_squares, squares.at[z], square_send.at[d], square_recv.at[d], (me, peer))

    barrier = pltpu.get_barrier_semaphore()
    each_peer(lambda d, p: pl.semaphore_signal(barrier, inc=1, device_id=(p, z), device_id_type=MESH))
    each_z(lambda d, p: pl.semaphore_signal(barrier, inc=1, device_id=(me, p), device_id_type=MESH))

    own_cache_copy = pltpu.make_async_copy(strip(cache, me), part(pieces, me), local_sem.at[0])
    own_cache_copy.start()
    none = pieces.shape[0] - 8
    pieces[pl.ds(none, 8)] = jnp.zeros((8, rows, LANES), F32)
    lane = lax.broadcasted_iota(jnp.int32, (1, LANES), 1)
    table = jnp.zeros((1, LANES), jnp.int32)
    for r in range(count):
        hit, write = hit_entry[r], write_entry[r]
        hit_slot = jnp.where(hit >= 0, entry_slot[jnp.maximum(hit, 0)], none)
        write_slot = jnp.where(write >= 0, entry_slot[jnp.maximum(write, 0)], -1)
        table = jnp.where(lane == HIT + r, hit_slot, table)
        table = jnp.where(lane == WRITE + r, write_slot, table)
    own_slots[...] = table
    slots[me] = table
    pl.semaphore_wait(barrier, n - 1 + nz - 1)

    each_peer(lambda d, p: slot_copy(d, p).start())
    each_peer(lambda d, p: cache_copy(d, p).start())

    low = lax.broadcasted_iota(jnp.int32, (length, length), 0)
    col = lax.broadcasted_iota(jnp.int32, (length, length), 1)
    causal = low >= col
    lower, upper = jnp.where(causal, 1.0, 0.0), jnp.where(low <= col, 1.0, 0.0)

    def block(r, decay_row):
        steps = log_decay[r]
        high = dict(precision=lax.Precision.HIGHEST)
        gsum_rows = jnp.dot(steps, upper, preferred_element_type=F32, **high)
        gsum_cols = nt(lower, steps, **high)
        last = gsum_rows[:, length - 1 : length]
        grown = jnp.exp(gsum_cols)
        for h in range(head_count):
            cols = slice(h * size, (h + 1) * size)
            q, k, v = queries[r, :, cols], key_rows[r, :, cols], values[r, :, cols]
            gcol, grow, glast = gsum_cols[:, h : h + 1], gsum_rows[h : h + 1], last[h : h + 1]
            gap = jnp.where(causal, jnp.exp(jnp.minimum(gcol - grow, 0.0)), 0.0)
            weights = (nt(q, k) * gap).astype(BF16)
            heads[r, :, cols] = jnp.dot(weights, v, preferred_element_type=F32)
            weighted = (k.astype(F32) * jnp.exp(glast - gcol)).astype(BF16)
            kv[r, h * size : (h + 1) * size, :] = tn(weighted, v)
            decay_cols[r, :, cols] = jnp.broadcast_to(grown[:, h : h + 1], (length, size))
            decay_row = jnp.where(lane == r * head_count + h, jnp.exp(glast), decay_row)
        return decay_row

    decay_row = lax.fori_loop(0, count, block, jnp.zeros((1, LANES), F32))
    own_decay[...] = decay_row
    decays[me] = decay_row
    own_kv_copy = pltpu.make_async_copy(strip(kv, me), part(kv_pieces, me), local_sem.at[1])
    own_kv_copy.start()
    each_peer(lambda d, p: decay_copy(d, p).start())
    each_peer(lambda d, p: kv_copy(d, p).start())

    each_peer(lambda d, p: slot_copy(d, p).wait_recv())
    to_scalar = pltpu.make_async_copy(slots, slots_s, local_sem.at[2])
    to_scalar.start()
    to_scalar.wait()
    place = (
        lax.broadcasted_iota(jnp.int32, (8, LANES), 0) * LANES
        + lax.broadcasted_iota(jnp.int32, (8, LANES), 1)
    )

    def invert(device, found):
        for r in range(count):
            found = jnp.where(place == slots_s[device, 0, WRITE + r], device * 16 + r + 1, found)
        return found

    inverse[...] = lax.fori_loop(0, n, invert, jnp.zeros((8, LANES), jnp.int32))
    to_scalar = pltpu.make_async_copy(inverse, inverse_s, local_sem.at[3])
    to_scalar.start()
    to_scalar.wait()

    own_cache_copy.wait()
    each_peer(lambda d, p: cache_copy(d, p).wait_recv())

    def pick(device, carry):
        for r in range(count):
            hit_pieces[device * count + r] = pieces[slots_s[device, 0, HIT + r]]
        return carry

    lax.fori_loop(0, n, pick, 0)
    own_hit_copy = pltpu.make_async_copy(part(hit_pieces, me), strip(prefix, me), local_sem.at[4])
    own_hit_copy.start()
    each_peer(lambda d, p: hit_copy(d, p).start())

    each_peer(lambda d, p: decay_copy(d, p).wait_recv())
    to_scalar = pltpu.make_async_copy(decays, decays_s, local_sem.at[5])
    to_scalar.start()
    to_scalar.wait()
    own_kv_copy.wait()
    each_peer(lambda d, p: kv_copy(d, p).wait_recv())
    my_head = (me * rows) // size

    def renew(device, carry):
        for e in range(count):
            slot = device * count + e
            code = inverse_s[slot // LANES, slot % LANES]
            writer = jnp.maximum(code - 1, 0)
            source, r = writer // 16, writer % 16
            state = decays_s[source, 0, r * head_count + my_head] * pieces[slots_s[source, 0, HIT + r]]
            state = state + kv_pieces[source * count + r]
            new_pieces[slot] = jnp.where(code > 0, state, pieces[slot])
        return carry

    lax.fori_loop(0, n, renew, 0)
    own_new_copy = pltpu.make_async_copy(part(new_pieces, me), strip(new_cache, me), local_sem.at[6])
    own_new_copy.start()
    each_peer(lambda d, p: new_copy(d, p).start())

    own_hit_copy.wait()
    each_peer(lambda d, p: hit_copy(d, p).wait_recv())
    lane_wide = lax.broadcasted_iota(jnp.int32, (length, LANES), 1)

    def carry_in(r, sums):
        total = jnp.zeros((length, 1), F32)
        for h in range(head_count):
            cols = slice(h * size, (h + 1) * size)
            state = prefix[r, h * size : (h + 1) * size, :]
            state_high = state.astype(BF16)
            state_low = (state - state_high.astype(F32)).astype(BF16)
            q = queries[r, :, cols]
            carried = jnp.dot(q, state_high, preferred_element_type=F32)
            carried = carried + jnp.dot(q, state_low, preferred_element_type=F32)
            out = heads[r, :, cols] + carried * decay_cols[r, :, cols]
            heads[r, :, cols] = out
            total = total + jnp.sum(out * out, axis=1, keepdims=True)
        return jnp.where(lane_wide == r, total, sums)

    sums = lax.fori_loop(0, count, carry_in, jnp.zeros((length, LANES), F32))
    flat = jnp.transpose(sums)
    packed = jnp.concatenate([flat[0:8], flat[8:16]], axis=1)
    own_squares[...] = packed
    squares[z] = packed
    each_z(lambda d, p: square_copy(d, p).start())
    each_z(lambda d, p: square_copy(d, p).wait_recv())
    total = jnp.sum(squares[...], axis=0)
    inv = lax.rsqrt(total / (width * nz) + 1e-06)
    inv = jnp.transpose(inv)

    def norm(r, carry):
        low_half = jnp.sum(jnp.where(lane8 == r, inv[0:length], 0.0), axis=1, keepdims=True)
        high_half = jnp.sum(jnp.where(lane8 == r - 8, inv[length:], 0.0), axis=1, keepdims=True)
        scale = low_half + high_half
        attended[r] = (heads[r] * scale * gain[...]).astype(BF16)
        return carry

    lane8 = lax.broadcasted_iota(jnp.int32, (length, 8), 1)
    lax.fori_loop(0, count, norm, 0)

    own_new_copy.wait()
    each_peer(lambda d, p: new_copy(d, p).wait_recv())
    each_peer(lambda d, p: slot_copy(d, p).wait_send())
    each_peer(lambda d, p: decay_copy(d, p).wait_send())
    each_peer(lambda d, p: cache_copy(d, p).wait_send())
    each_peer(lambda d, p: kv_copy(d, p).wait_send())
    each_peer(lambda d, p: hit_copy(d, p).wait_send())
    each_peer(lambda d, p: new_copy(d, p).wait_send())
    each_z(lambda d, p: square_copy(d, p).wait_send())


def body(
    n, nz, queries, key_rows, values, log_decay, state_cache, norm_gain, entry_slot, hit_entry, write_entry
):
    count, length, width = queries.shape
    entries, head_count, size, _ = state_cache.shape
    tall = head_count * size
    rows = tall // n
    vmem, smem = pl.BlockSpec(memory_space=pltpu.VMEM), pl.BlockSpec(memory_space=pltpu.SMEM)
    anywhere = pl.BlockSpec(memory_space=pl.ANY)
    sem = pltpu.SemaphoreType.DMA
    attended, new_cache = pl.pallas_call(
        functools.partial(kernel, n, nz),
        out_shape=(
            jax.ShapeDtypeStruct((count, length, width), BF16),
            jax.ShapeDtypeStruct((entries, tall, size), F32),
        ),
        in_specs=[smem, smem, smem, vmem, vmem, vmem, vmem, vmem, anywhere],
        out_specs=(vmem, anywhere),
        scratch_shapes=[
            pltpu.VMEM((n * entries + 8, rows, size), F32),
            pltpu.VMEM((n * count, rows, size), F32),
            pltpu.VMEM((count, tall, size), F32),
            pltpu.VMEM((n * count, rows, size), F32),
            pltpu.VMEM((n * entries, rows, size), F32),
            pltpu.VMEM((count, tall, size), F32),
            pltpu.VMEM((count, length, width), F32),
            pltpu.VMEM((count, length, width), F32),
            pltpu.VMEM((1, LANES), jnp.int32),
            pltpu.VMEM((n, 1, LANES), jnp.int32),
            pltpu.VMEM((1, LANES), F32),
            pltpu.VMEM((n, 1, LANES), F32),
            pltpu.VMEM((8, LANES), jnp.int32),
            pltpu.VMEM((8, LANES), F32),
            pltpu.VMEM((nz, 8, LANES), F32),
            pltpu.SMEM((n, 1, LANES), jnp.int32),
            pltpu.SMEM((n, 1, LANES), F32),
            pltpu.SMEM((8, LANES), jnp.int32),
            *[sem((n,))] * 12,
            sem((nz,)),
            sem((nz,)),
            sem((7,)),
        ],
        compiler_params=pltpu.CompilerParams(
            collective_id=0, has_side_effects=True, vmem_limit_bytes=32 << 20
        ),
    )(
        entry_slot, hit_entry, write_entry, log_decay, queries, key_rows, values,
        norm_gain.reshape(1, width), state_cache.reshape(entries, tall, size),
    )
    return attended, new_cache.reshape(state_cache.shape)


def solution(mesh):
    placed = (
        P("req", None, "head"),
        P("req", None, "head"),
        P("req", None, "head"),
        P("req", "head", None),
        P("req", "head", None, None),
        P("head"),
        P(),
        P("req"),
        P("req"),
    )
    return jax.shard_map(
        functools.partial(body, mesh.shape["req"], mesh.shape["head"]),
        mesh=mesh,
        in_specs=placed,
        out_specs=(P("req", None, "head"), P("req", "head", None, None)),
        check_vma=False,
    )
```

time: 314 us -> 115 us (0.37)
  the two profiles are of different devices: /device:TPU:4 before, /device:TPU:1 now
where the time goes in v1:
time: 115 us; the launch traced here: 114 us
  Pallas kernels  104 us (90%)
  local copies, waits for them, and re-layouts  9.65 us (8%)
    pallas_call x1, Pallas kernels, body(): pl.pallas_call(functools.partial(kernel, n, nz), out_shape=(jax.ShapeDtyp...  104 us
    unnamed x20, local copies, waits for them, and re-layouts  9.65 us

profile of v1, /device:TPU:1, one launch (start us, length us, event | category | flops | bytes accessed | tf_op | source)
XLA Modules:
  0.0 114.3 jit_solution(9713301388711727051)
XLA Ops:
  0.6 0.0 copy-start
  0.6 1.4 %copy-done = f32[12,2,128,128]{3,2,1,0:T(8,128)S(1)} copy-done((f32[12,2,128,128]{3,2,1,0:T(8,128)S(1)}, f32[12,2,128,128]{3,2,1,0:T(8,128)}, u32[]{:S(2)}) %copy-start) | copy-done | bytes 1572888
  2.0 0.0 copy-start.1
  2.0 1.0 copy-done.1
  3.0 0.0 copy-start.2
  3.0 1.0 copy-done.2
  4.0 0.0 copy-start.3
  4.0 1.0 copy-done.3
  5.0 0.0 copy-start.4
  5.0 0.7 copy-done.4
  5.7 0.0 copy-start.5
  5.7 0.7 copy-done.5
  6.4 0.0 copy-start.6
  6.4 0.7 copy-done.6
  7.1 0.0 copy-start.7
  7.1 0.7 copy-done.7
  7.8 0.0 copy-start.8
  7.8 0.7 copy-done.8
  8.4 104.0 %shard_map.104 = (bf16[12,64,256]{2,1,0:T(8,128)(2,1)S(1)}, f32[12,256,128]{2,1,0:T(8,128)S(1)}) custom-call(s32[384]{0:T(512)S(1)} %copy-done.5, s32[12]{0:T(128)S(1)} %copy-done.7, s32[12]{0:T(128)S(1)} %copy-done.8, f32[12,2,64]{2,1,0:T(2,128)S(1)} %copy-done.4, bf16[12,64,256]{2,1,0:T(8,128)(2,1)S(1)} %copy-done.1, bf16[12,64,256]{2,1,0:T(8,128)(2,1)S(1)} %copy-done.2, ...), custom_call_target="tpu_custom_call" | custom-call | tf_op jit(solution)/shard_map/pallas_call | solution.py:262
  112.4 0.7 copy.13
  113.2 1.1 copy.14
Async XLA Ops:
  0.6 1.4 %copy-start = (f32[12,2,128,128]{3,2,1,0:T(8,128)S(1)}, f32[12,2,128,128]{3,2,1,0:T(8,128)}, u32[]{:S(2)}) copy-start(f32[12,2,128,128]{3,2,1,0:T(8,128)} %param.13) | copy-start | bytes 4718596
  2.0 1.0 copy-start.1
  3.0 1.0 copy-start.2
  4.0 1.0 copy-start.3
  5.0 0.7 copy-start.4
  5.7 0.7 copy-start.5
  6.4 0.7 copy-start.6
  7.1 0.7 copy-start.7
  7.8 0.7 copy-start.8

commit v2 on v1

--- a/solution.py
+++ b/solution.py
@@ -12,6 +12,7 @@
 BF16 = jnp.bfloat16
 LANES = 128
 HIT, WRITE = 0, 16
+STRIDE = 5
 
 
 def nt(a, b, **kw):
@@ -23,12 +24,13 @@
 
 
 def kernel(
-    n, nz, entry_slot, hit_entry, write_entry, log_decay, queries, key_rows, values, gain, cache,
+    n, nz, slot_hbm, hit_hbm, write_hbm, log_decay_hbm, queries_hbm, key_rows_hbm, values_hbm, gain_hbm, cache,
     attended, new_cache,
     pieces, kv_pieces, kv, hit_pieces, new_pieces, prefix, heads, decay_cols, own_slots, slots,
-    own_decay, decays, inverse, own_squares, squares, slots_s, decays_s, inverse_s,
+    own_decay, decays, source_rows, source_decay, own_squares, squares, log_decay, queries, key_rows, values, gain,
+    slots_s, decays_s, source_rows_s, source_decay_s, entry_slot, hit_entry, write_entry,
     slot_send, slot_recv, decay_send, decay_recv, cache_send, cache_recv, kv_send, kv_recv,
-    hit_send, hit_recv, new_send, new_recv, square_send, square_recv, local_sem,
+    hit_send, hit_recv, new_send, new_recv, square_send, square_recv, local_sem, plane_in, planes_in,
 ):
     count, length, width = queries.shape
     head_count = log_decay.shape[1]
@@ -40,12 +42,13 @@
         x, y, c = me // 8, (me // 2) % 4, me % 2
         return ((x + d // 8) % 4) * 8 + ((y + (d // 2) % 4) % 4) * 2 + (c + d % 2) % 2
 
-    def each_peer(act):
-        def step(d, carry):
+    def each_peer(act, low=1, high=n):
+        def step(i, carry):
+            d = (i * STRIDE) % n
             act(d, peer_of(d))
             return carry
 
-        lax.fori_loop(1, n, step, 0)
+        lax.fori_loop(low, high, step, 0)
 
     def each_z(act):
         def step(d, carry):
@@ -87,34 +90,84 @@
         return remote(own_squares, squares.at[z], square_send.at[d], square_recv.at[d], (me, peer))
 
     barrier = pltpu.get_barrier_semaphore()
-    each_peer(lambda d, p: pl.semaphore_signal(barrier, inc=1, device_id=(p, z), device_id_type=MESH))
-    each_z(lambda d, p: pl.semaphore_signal(barrier, inc=1, device_id=(me, p), device_id_type=MESH))
-
-    own_cache_copy = pltpu.make_async_copy(strip(cache, me), part(pieces, me), local_sem.at[0])
-    own_cache_copy.start()
-    none = pieces.shape[0] - 8
+    last = n - 1
+
+    def signal(semaphore, device):
+        pl.semaphore_signal(semaphore, inc=1, device_id=device, device_id_type=MESH)
+
+    def greet(d, p):
+        @pl.when(p != last)
+        def _():
+            signal(barrier, (p, z))
+
+    each_peer(greet)
+
+    def fetch(src, dst, k):
+        copy = pltpu.make_async_copy(src, dst, local_sem.at[k])
+        copy.start()
+        return copy
+
+    tables_in = [
+        fetch(hit_hbm, hit_entry, 0),
+        fetch(write_hbm, write_entry, 1),
+        fetch(slot_hbm, entry_slot, 2),
+        fetch(log_decay_hbm, log_decay, 3),
+    ]
+    rows_in = [
+        fetch(queries_hbm, queries, 4),
+        fetch(key_rows_hbm, key_rows, 5),
+        fetch(values_hbm, values, 6),
+        fetch(gain_hbm, gain, 7),
+    ]
+    own_cache_copy = fetch(strip(cache, me), part(pieces, me), 8)
+    none = n * count
     pieces[pl.ds(none, 8)] = jnp.zeros((8, rows, LANES), F32)
+    kv_pieces[pl.ds(none, 8)] = jnp.zeros((8, rows, LANES), F32)
+
+    @pl.when(me != last)
+    def _():
+        pl.semaphore_wait(barrier, n - 1)
+
+    @pl.when(me == last - 1)
+    def _():
+        signal(plane_in, (last, z))
+
+    @pl.when(me == last)
+    def _():
+        pl.semaphore_wait(plane_in, 1)
+        each_z(lambda d, p: signal(barrier, (me, p)))
+
+    each_peer(lambda d, p: cache_copy(d, p).start(), 1, n // 4)
+    for copy in tables_in:
+        copy.wait()
     lane = lax.broadcasted_iota(jnp.int32, (1, LANES), 1)
     table = jnp.zeros((1, LANES), jnp.int32)
+    decay_row = jnp.zeros((1, LANES), F32)
     for r in range(count):
         hit, write = hit_entry[r], write_entry[r]
         hit_slot = jnp.where(hit >= 0, entry_slot[jnp.maximum(hit, 0)], none)
         write_slot = jnp.where(write >= 0, entry_slot[jnp.maximum(write, 0)], -1)
         table = jnp.where(lane == HIT + r, hit_slot, table)
         table = jnp.where(lane == WRITE + r, write_slot, table)
+        whole = jnp.exp(jnp.sum(log_decay[r], axis=1, keepdims=True))
+        for h in range(head_count):
+            decay_row = jnp.where(lane == r * head_count + h, whole[h : h + 1], decay_row)
     own_slots[...] = table
     slots[me] = table
-    pl.semaphore_wait(barrier, n - 1 + nz - 1)
-
+    own_decay[...] = decay_row
+    decays[me] = decay_row
     each_peer(lambda d, p: slot_copy(d, p).start())
-    each_peer(lambda d, p: cache_copy(d, p).start())
+    each_peer(lambda d, p: decay_copy(d, p).start())
+    each_peer(lambda d, p: cache_copy(d, p).start(), n // 4, n)
+    for copy in rows_in:
+        copy.wait()
 
     low = lax.broadcasted_iota(jnp.int32, (length, length), 0)
     col = lax.broadcasted_iota(jnp.int32, (length, length), 1)
     causal = low >= col
     lower, upper = jnp.where(causal, 1.0, 0.0), jnp.where(low <= col, 1.0, 0.0)
 
-    def block(r, decay_row):
+    def block(r, carry):
         steps = log_decay[r]
         high = dict(precision=lax.Precision.HIGHEST)
         gsum_rows = jnp.dot(steps, upper, preferred_element_type=F32, **high)
@@ -131,72 +184,86 @@
             weighted = (k.astype(F32) * jnp.exp(glast - gcol)).astype(BF16)
             kv[r, h * size : (h + 1) * size, :] = tn(weighted, v)
             decay_cols[r, :, cols] = jnp.broadcast_to(grown[:, h : h + 1], (length, size))
-            decay_row = jnp.where(lane == r * head_count + h, jnp.exp(glast), decay_row)
-        return decay_row
-
-    decay_row = lax.fori_loop(0, count, block, jnp.zeros((1, LANES), F32))
-    own_decay[...] = decay_row
-    decays[me] = decay_row
-    own_kv_copy = pltpu.make_async_copy(strip(kv, me), part(kv_pieces, me), local_sem.at[1])
-    own_kv_copy.start()
-    each_peer(lambda d, p: decay_copy(d, p).start())
-    each_peer(lambda d, p: kv_copy(d, p).start())
+        return carry
+
+    lax.fori_loop(0, count, block, 0)
 
     each_peer(lambda d, p: slot_copy(d, p).wait_recv())
-    to_scalar = pltpu.make_async_copy(slots, slots_s, local_sem.at[2])
-    to_scalar.start()
-    to_scalar.wait()
+    each_peer(lambda d, p: decay_copy(d, p).wait_recv())
+    for copy in [fetch(slots, slots_s, 9), fetch(decays, decays_s, 10)]:
+        copy.wait()
     place = (
         lax.broadcasted_iota(jnp.int32, (8, LANES), 0) * LANES
         + lax.broadcasted_iota(jnp.int32, (8, LANES), 1)
     )
+    my_head = (me * rows) // size
 
     def invert(device, found):
+        hit_row, kv_row, decay = found
         for r in range(count):
-            found = jnp.where(place == slots_s[device, 0, WRITE + r], device * 16 + r + 1, found)
-        return found
-
-    inverse[...] = lax.fori_loop(0, n, invert, jnp.zeros((8, LANES), jnp.int32))
-    to_scalar = pltpu.make_async_copy(inverse, inverse_s, local_sem.at[3])
-    to_scalar.start()
-    to_scalar.wait()
+            here = place == slots_s[device, 0, WRITE + r]
+            hit_row = jnp.where(here, slots_s[device, 0, HIT + r], hit_row)
+            kv_row = jnp.where(here, device * count + r, kv_row)
+            decay = jnp.where(here, decays_s[device, 0, r * head_count + my_head], decay)
+        return hit_row, kv_row, decay
+
+    hit_row, kv_row, decay = lax.fori_loop(
+        0, n, invert, (place, jnp.full((8, LANES), none, jnp.int32), jnp.ones((8, LANES), F32))
+    )
+    source_rows[0] = hit_row
+    source_rows[1] = kv_row
+    source_decay[...] = decay
+    sources_in = [fetch(source_rows, source_rows_s, 11), fetch(source_decay, source_decay_s, 12)]
+
+    own_kv_copy = fetch(strip(kv, me), part(kv_pieces, me), 13)
+
+    def send_kv(d, p):
+        cache_copy(d, p).wait_send()
+        kv_copy(d, p).start()
+
+    each_peer(send_kv)
 
     own_cache_copy.wait()
     each_peer(lambda d, p: cache_copy(d, p).wait_recv())
 
-    def pick(device, carry):
+    def pick(device):
         for r in range(count):
             hit_pieces[device * count + r] = pieces[slots_s[device, 0, HIT + r]]
-        return carry
-
-    lax.fori_loop(0, n, pick, 0)
-    own_hit_copy = pltpu.make_async_copy(part(hit_pieces, me), strip(prefix, me), local_sem.at[4])
-    own_hit_copy.start()
-    each_peer(lambda d, p: hit_copy(d, p).start())
-
-    each_peer(lambda d, p: decay_copy(d, p).wait_recv())
-    to_scalar = pltpu.make_async_copy(decays, decays_s, local_sem.at[5])
-    to_scalar.start()
-    to_scalar.wait()
+
+    def send_hits(d, p):
+        pick(p)
+        kv_copy(d, p).wait_send()
+        hit_copy(d, p).start()
+
+    each_peer(send_hits)
+    pick(me)
+    own_hit_copy = fetch(part(hit_pieces, me), strip(prefix, me), 14)
+
+    @pl.when(me == last)
+    def _():
+        pl.semaphore_wait(barrier, nz - 1)
+        each_peer(lambda d, p: signal(planes_in, (p, z)))
+
     own_kv_copy.wait()
     each_peer(lambda d, p: kv_copy(d, p).wait_recv())
-    my_head = (me * rows) // size
-
-    def renew(device, carry):
+    for copy in sources_in:
+        copy.wait()
+
+    def renew(device):
         for e in range(count):
             slot = device * count + e
-            code = inverse_s[slot // LANES, slot % LANES]
-            writer = jnp.maximum(code - 1, 0)
-            source, r = writer // 16, writer % 16
-            state = decays_s[source, 0, r * head_count + my_head] * pieces[slots_s[source, 0, HIT + r]]
-            state = state + kv_pieces[source * count + r]
-            new_pieces[slot] = jnp.where(code > 0, state, pieces[slot])
-        return carry
-
-    lax.fori_loop(0, n, renew, 0)
-    own_new_copy = pltpu.make_async_copy(part(new_pieces, me), strip(new_cache, me), local_sem.at[6])
-    own_new_copy.start()
-    each_peer(lambda d, p: new_copy(d, p).start())
+            sub, at = slot // LANES, slot % LANES
+            state = source_decay_s[sub, at] * pieces[source_rows_s[0, sub, at]]
+            new_pieces[slot] = state + kv_pieces[source_rows_s[1, sub, at]]
+
+    def send_new(d, p):
+        renew(p)
+        hit_copy(d, p).wait_send()
+        new_copy(d, p).start()
+
+    each_peer(send_new)
+    renew(me)
+    own_new_copy = fetch(part(new_pieces, me), strip(new_cache, me), 15)
 
     own_hit_copy.wait()
     each_peer(lambda d, p: hit_copy(d, p).wait_recv())
@@ -222,6 +289,11 @@
     packed = jnp.concatenate([flat[0:8], flat[8:16]], axis=1)
     own_squares[...] = packed
     squares[z] = packed
+
+    @pl.when(me != last)
+    def _():
+        pl.semaphore_wait(planes_in, 1)
+
     each_z(lambda d, p: square_copy(d, p).start())
     each_z(lambda d, p: square_copy(d, p).wait_recv())
     total = jnp.sum(squares[...], axis=0)
@@ -242,9 +314,6 @@
     each_peer(lambda d, p: new_copy(d, p).wait_recv())
     each_peer(lambda d, p: slot_copy(d, p).wait_send())
     each_peer(lambda d, p: decay_copy(d, p).wait_send())
-    each_peer(lambda d, p: cache_copy(d, p).wait_send())
-    each_peer(lambda d, p: kv_copy(d, p).wait_send())
-    each_peer(lambda d, p: hit_copy(d, p).wait_send())
     each_peer(lambda d, p: new_copy(d, p).wait_send())
     each_z(lambda d, p: square_copy(d, p).wait_send())
 
@@ -256,20 +325,19 @@
     entries, head_count, size, _ = state_cache.shape
     tall = head_count * size
     rows = tall // n
-    vmem, smem = pl.BlockSpec(memory_space=pltpu.VMEM), pl.BlockSpec(memory_space=pltpu.SMEM)
-    anywhere = pl.BlockSpec(memory_space=pl.ANY)
+    vmem, hbm = pl.BlockSpec(memory_space=pltpu.VMEM), pl.BlockSpec(memory_space=pltpu.HBM)
     sem = pltpu.SemaphoreType.DMA
     attended, new_cache = pl.pallas_call(
         functools.partial(kernel, n, nz),
         out_shape=(
-            jax.ShapeDtypeStruct((count, length, width), BF16),
-            jax.ShapeDtypeStruct((entries, tall, size), F32),
+            pltpu.VMEM((count, length, width), BF16),
+            pltpu.VMEM((entries, tall, size), F32),
         ),
-        in_specs=[smem, smem, smem, vmem, vmem, vmem, vmem, vmem, anywhere],
-        out_specs=(vmem, anywhere),
+        in_specs=[hbm] * 9,
+        out_specs=(vmem, vmem),
         scratch_shapes=[
             pltpu.VMEM((n * entries + 8, rows, size), F32),
-            pltpu.VMEM((n * count, rows, size), F32),
+            pltpu.VMEM((n * count + 8, rows, size), F32),
             pltpu.VMEM((count, tall, size), F32),
             pltpu.VMEM((n * count, rows, size), F32),
             pltpu.VMEM((n * entries, rows, size), F32),
@@ -280,23 +348,38 @@
             pltpu.VMEM((n, 1, LANES), jnp.int32),
             pltpu.VMEM((1, LANES), F32),
             pltpu.VMEM((n, 1, LANES), F32),
-            pltpu.VMEM((8, LANES), jnp.int32),
+            pltpu.VMEM((2, 8, LANES), jnp.int32),
+            pltpu.VMEM((8, LANES), F32),
             pltpu.VMEM((8, LANES), F32),
             pltpu.VMEM((nz, 8, LANES), F32),
+            pltpu.VMEM(log_decay.shape, F32),
+            *[pltpu.VMEM((count, length, width), BF16)] * 3,
+            pltpu.VMEM((1, width), F32),
             pltpu.SMEM((n, 1, LANES), jnp.int32),
             pltpu.SMEM((n, 1, LANES), F32),
-            pltpu.SMEM((8, LANES), jnp.int32),
+            pltpu.SMEM((2, 8, LANES), jnp.int32),
+            pltpu.SMEM((8, LANES), F32),
+            pltpu.SMEM(entry_slot.shape, jnp.int32),
+            pltpu.SMEM(hit_entry.shape, jnp.int32),
+            pltpu.SMEM(write_entry.shape, jnp.int32),
             *[sem((n,))] * 12,
             sem((nz,)),
             sem((nz,)),
-            sem((7,)),
+            sem((16,)),
+            pltpu.SemaphoreType.REGULAR,
+            pltpu.SemaphoreType.REGULAR,
         ],
         compiler_params=pltpu.CompilerParams(
             collective_id=0, has_side_effects=True, vmem_limit_bytes=32 << 20
         ),
     )(
-        entry_slot, hit_entry, write_entry, log_decay, queries, key_rows, values,
-        norm_gain.reshape(1, width), state_cache.reshape(entries, tall, size),
+        *(
+            pltpu.with_memory_space_constraint(x, pltpu.HBM)
+            for x in (
+                entry_slot, hit_entry, write_entry, log_decay, queries, key_rows, values,
+                norm_gain.reshape(1, width), state_cache.reshape(entries, tall, size),
+            )
+        )
     )
     return attended, new_cache.reshape(state_cache.shape)
 

time: 115 us -> 93 us (0.81)
  Pallas kernels: 104 us -> 90.3 us
  local copies, waits for them, and re-layouts: 9.65 us -> 1.89 us
    pallas_call x1, Pallas kernels: 104 us -> 90.3 us  [body(): pl.pallas_call(functools.partial(kernel, n, nz), out_shape=(pltpu.VMEM((c...]
    unnamed x20 -> x2, local copies, waits for them, and re-layouts: 9.65 us -> 1.89 us
where the time goes in v2:
time: 93 us; the launch traced here: 92.9 us
  Pallas kernels  90.3 us (97%)
  local copies, waits for them, and re-layouts  1.89 us (2%)
    pallas_call x1, Pallas kernels, body(): pl.pallas_call(functools.partial(kernel, n, nz), out_shape=(pltpu.VMEM((c...  90.3 us
    unnamed x2, local copies, waits for them, and re-layouts  1.89 us

profile of v2, /device:TPU:1, one launch (start us, length us, event | category | flops | bytes accessed | tf_op | source)
XLA Modules:
  0.0 92.9 jit_solution(4891021994860561374)
XLA Ops:
  0.6 90.3 %shard_map.104 = (bf16[12,64,256]{2,1,0:T(8,128)(2,1)S(1)}, f32[12,256,128]{2,1,0:T(8,128)S(1)}) custom-call(s32[384]{0:T(512)} %slot_hbm.1, s32[12]{0:T(128)} %hit_hbm.1, s32[12]{0:T(128)} %write_hbm.1, f32[12,2,64]{2,1,0:T(2,128)} %log_decay_hbm.1, bf16[12,64,256]{2,1,0:T(8,128)(2,1)} %queries_hbm.1, bf16[12,64,256]{2,1,0:T(8,128)(2,1)} %key_rows_hbm.1, ...), custom_call_target="tpu_custom_call" | custom-call | tf_op jit(solution)/shard_map/pallas_call | solution.py:330
  91.0 0.7 copy.13
  91.7 1.1 %copy.14 = f32[12,2,128,128]{3,2,1,0:T(8,128)} copy(f32[12,2,128,128]{3,2,1,0:T(8,128)S(1)} %bitcast.3) | data formatting | bytes 3145728

commit v3 on v2

--- a/solution.py
+++ b/solution.py
@@ -38,21 +38,23 @@
     rows = cache.shape[1] // n
     me, z = lax.axis_index("req"), lax.axis_index("head")
 
-    def peer_of(d):
-        x, y, c = me // 8, (me // 2) % 4, me % 2
-        return ((x + d // 8) % 4) * 8 + ((y + (d // 2) % 4) % 4) * 2 + (c + d % 2) % 2
+    core = lax.rem(me, 2)
+    y2 = lax.rem(me, 8) - core
+    x8 = me - lax.rem(me, 8)
 
     def each_peer(act, low=1, high=n):
         def step(i, carry):
-            d = (i * STRIDE) % n
-            act(d, peer_of(d))
+            d = lax.rem(i * STRIDE, n)
+            within = lax.rem(d, 8)
+            side = lax.rem(d, 2)
+            act(lax.rem(x8 + d - within, n) + lax.rem(y2 + within - side, 8) + lax.rem(core + side, 2))
             return carry
 
         lax.fori_loop(low, high, step, 0)
 
     def each_z(act):
         def step(d, carry):
-            act(d, lax.rem(z + d, nz))
+            act(lax.rem(z + d, nz))
             return carry
 
         lax.fori_loop(1, nz, step, 0)
@@ -68,26 +70,32 @@
     def strip(ref, device):
         return ref.at[:, pl.ds(pl.multiple_of(device * rows, rows), rows), :]
 
-    def slot_copy(d, peer):
-        return remote(own_slots, slots.at[me], slot_send.at[d], slot_recv.at[d], (peer, z))
-
-    def decay_copy(d, peer):
-        return remote(own_decay, decays.at[me], decay_send.at[d], decay_recv.at[d], (peer, z))
-
-    def cache_copy(d, peer):
-        return remote(strip(cache, peer), part(pieces, me), cache_send.at[d], cache_recv.at[d], (peer, z))
-
-    def kv_copy(d, peer):
-        return remote(strip(kv, peer), part(kv_pieces, me), kv_send.at[d], kv_recv.at[d], (peer, z))
-
-    def hit_copy(d, peer):
-        return remote(part(hit_pieces, peer), strip(prefix, me), hit_send.at[d], hit_recv.at[d], (peer, z))
-
-    def new_copy(d, peer):
-        return remote(part(new_pieces, peer), strip(new_cache, me), new_send.at[d], new_recv.at[d], (peer, z))
-
-    def square_copy(d, peer):
-        return remote(own_squares, squares.at[z], square_send.at[d], square_recv.at[d], (me, peer))
+    def slot_copy(peer):
+        return remote(own_slots, slots.at[me], slot_send, slot_recv, (peer, z))
+
+    def decay_copy(peer):
+        return remote(own_decay, decays.at[me], decay_send, decay_recv, (peer, z))
+
+    def cache_copy(peer):
+        return remote(strip(cache, peer), part(pieces, me), cache_send, cache_recv, (peer, z))
+
+    def kv_copy(peer):
+        return remote(strip(kv, peer), part(kv_pieces, me), kv_send, kv_recv, (peer, z))
+
+    def hit_copy(peer):
+        return remote(part(hit_pieces, peer), strip(prefix, me), hit_send, hit_recv, (peer, z))
+
+    def new_copy(peer):
+        return remote(part(new_pieces, peer), strip(new_cache, me), new_send, new_recv, (peer, z))
+
+    def square_copy(peer):
+        return remote(own_squares, squares.at[z], square_send, square_recv, (me, peer))
+
+    def await_all(ref, semaphore, amount):
+        whole = ref.at[pl.ds(0, amount)]
+        pltpu.make_async_copy(whole, whole, semaphore).wait()
+
+    others, other_pieces = n - 1, (n - 1) * count
 
     barrier = pltpu.get_barrier_semaphore()
     last = n - 1
@@ -95,7 +103,7 @@
     def signal(semaphore, device):
         pl.semaphore_signal(semaphore, inc=1, device_id=device, device_id_type=MESH)
 
-    def greet(d, p):
+    def greet(p):
         @pl.when(p != last)
         def _():
             signal(barrier, (p, z))
@@ -135,9 +143,9 @@
     @pl.when(me == last)
     def _():
         pl.semaphore_wait(plane_in, 1)
-        each_z(lambda d, p: signal(barrier, (me, p)))
-
-    each_peer(lambda d, p: cache_copy(d, p).start(), 1, n // 4)
+        each_z(lambda p: signal(barrier, (me, p)))
+
+    each_peer(lambda p: cache_copy(p).start(), 1, n // 4)
     for copy in tables_in:
         copy.wait()
     lane = lax.broadcasted_iota(jnp.int32, (1, LANES), 1)
@@ -156,9 +164,9 @@
     slots[me] = table
     own_decay[...] = decay_row
     decays[me] = decay_row
-    each_peer(lambda d, p: slot_copy(d, p).start())
-    each_peer(lambda d, p: decay_copy(d, p).start())
-    each_peer(lambda d, p: cache_copy(d, p).start(), n // 4, n)
+    each_peer(lambda p: slot_copy(p).start())
+    each_peer(lambda p: decay_copy(p).start())
+    each_peer(lambda p: cache_copy(p).start(), n // 4, n)
     for copy in rows_in:
         copy.wait()
 
@@ -187,9 +195,12 @@
         return carry
 
     lax.fori_loop(0, count, block, 0)
-
-    each_peer(lambda d, p: slot_copy(d, p).wait_recv())
-    each_peer(lambda d, p: decay_copy(d, p).wait_recv())
+    own_kv_copy = fetch(strip(kv, me), part(kv_pieces, me), 13)
+
+    each_peer(lambda p: kv_copy(p).start())
+
+    await_all(slots, slot_recv, others)
+    await_all(decays, decay_recv, others)
     for copy in [fetch(slots, slots_s, 9), fetch(decays, decays_s, 10)]:
         copy.wait()
     place = (
@@ -215,25 +226,17 @@
     source_decay[...] = decay
     sources_in = [fetch(source_rows, source_rows_s, 11), fetch(source_decay, source_decay_s, 12)]
 
-    own_kv_copy = fetch(strip(kv, me), part(kv_pieces, me), 13)
-
-    def send_kv(d, p):
-        cache_copy(d, p).wait_send()
-        kv_copy(d, p).start()
-
-    each_peer(send_kv)
 
     own_cache_copy.wait()
-    each_peer(lambda d, p: cache_copy(d, p).wait_recv())
+    await_all(pieces, cache_recv, other_pieces)
 
     def pick(device):
         for r in range(count):
             hit_pieces[device * count + r] = pieces[slots_s[device, 0, HIT + r]]
 
-    def send_hits(d, p):
+    def send_hits(p):
         pick(p)
-        kv_copy(d, p).wait_send()
-        hit_copy(d, p).start()
+        hit_copy(p).start()
 
     each_peer(send_hits)
     pick(me)
@@ -242,31 +245,30 @@
     @pl.when(me == last)
     def _():
         pl.semaphore_wait(barrier, nz - 1)
-        each_peer(lambda d, p: signal(planes_in, (p, z)))
+        each_peer(lambda p: signal(planes_in, (p, z)))
 
     own_kv_copy.wait()
-    each_peer(lambda d, p: kv_copy(d, p).wait_recv())
+    await_all(kv_pieces, kv_recv, other_pieces)
     for copy in sources_in:
         copy.wait()
 
     def renew(device):
         for e in range(count):
             slot = device * count + e
-            sub, at = slot // LANES, slot % LANES
+            sub, at = lax.div(slot, LANES), lax.rem(slot, LANES)
             state = source_decay_s[sub, at] * pieces[source_rows_s[0, sub, at]]
             new_pieces[slot] = state + kv_pieces[source_rows_s[1, sub, at]]
 
-    def send_new(d, p):
+    def send_new(p):
         renew(p)
-        hit_copy(d, p).wait_send()
-        new_copy(d, p).start()
+        new_copy(p).start()
 
     each_peer(send_new)
     renew(me)
     own_new_copy = fetch(part(new_pieces, me), strip(new_cache, me), 15)
 
     own_hit_copy.wait()
-    each_peer(lambda d, p: hit_copy(d, p).wait_recv())
+    await_all(hit_pieces, hit_recv, other_pieces)
     lane_wide = lax.broadcasted_iota(jnp.int32, (length, LANES), 1)
 
     def carry_in(r, sums):
@@ -294,8 +296,8 @@
     def _():
         pl.semaphore_wait(planes_in, 1)
 
-    each_z(lambda d, p: square_copy(d, p).start())
-    each_z(lambda d, p: square_copy(d, p).wait_recv())
+    each_z(lambda p: square_copy(p).start())
+    await_all(squares, square_recv, nz - 1)
     total = jnp.sum(squares[...], axis=0)
     inv = lax.rsqrt(total / (width * nz) + 1e-06)
     inv = jnp.transpose(inv)
@@ -311,11 +313,14 @@
     lax.fori_loop(0, count, norm, 0)
 
     own_new_copy.wait()
-    each_peer(lambda d, p: new_copy(d, p).wait_recv())
-    each_peer(lambda d, p: slot_copy(d, p).wait_send())
-    each_peer(lambda d, p: decay_copy(d, p).wait_send())
-    each_peer(lambda d, p: new_copy(d, p).wait_send())
-    each_z(lambda d, p: square_copy(d, p).wait_send())
+    await_all(new_pieces, new_recv, other_pieces)
+    await_all(slots, slot_send, others)
+    await_all(decays, decay_send, others)
+    await_all(new_pieces, new_send, other_pieces)
+    await_all(pieces, cache_send, other_pieces)
+    await_all(kv_pieces, kv_send, other_pieces)
+    await_all(hit_pieces, hit_send, other_pieces)
+    await_all(squares, square_send, nz - 1)
 
 
 def body(
@@ -362,9 +367,7 @@
             pltpu.SMEM(entry_slot.shape, jnp.int32),
             pltpu.SMEM(hit_entry.shape, jnp.int32),
             pltpu.SMEM(write_entry.shape, jnp.int32),
-            *[sem((n,))] * 12,
-            sem((nz,)),
-            sem((nz,)),
+            *[sem] * 14,
             sem((16,)),
             pltpu.SemaphoreType.REGULAR,
             pltpu.SemaphoreType.REGULAR,

time: 93 us -> 86.3 us (0.928)
  Pallas kernels: 90.3 us -> 82.8 us
    pallas_call x1, Pallas kernels: 90.3 us -> 82.8 us  [body(): pl.pallas_call(functools.partial(kernel, n, nz), out_shape=(pltpu.VMEM((c...]
where the time goes in v3:
time: 86.3 us; the launch traced here: 85.4 us
  Pallas kernels  82.8 us (96%)
  local copies, waits for them, and re-layouts  1.89 us (2%)
    pallas_call x1, Pallas kernels, body(): pl.pallas_call(functools.partial(kernel, n, nz), out_shape=(pltpu.VMEM((c...  82.8 us
    unnamed x2, local copies, waits for them, and re-layouts  1.89 us

profile of v3, /device:TPU:1, one launch (start us, length us, event | category | flops | bytes accessed | tf_op | source)
XLA Modules:
  0.0 85.4 jit_solution(11499550503405510183)
XLA Ops:
  0.6 82.8 %shard_map.104 = (bf16[12,64,256]{2,1,0:T(8,128)(2,1)S(1)}, f32[12,256,128]{2,1,0:T(8,128)S(1)}) custom-call(s32[384]{0:T(512)} %slot_hbm.1, s32[12]{0:T(128)} %hit_hbm.1, s32[12]{0:T(128)} %write_hbm.1, f32[12,2,64]{2,1,0:T(2,128)} %log_decay_hbm.1, bf16[12,64,256]{2,1,0:T(8,128)(2,1)} %queries_hbm.1, bf16[12,64,256]{2,1,0:T(8,128)(2,1)} %key_rows_hbm.1, ...), custom_call_target="tpu_custom_call" | custom-call | tf_op jit(solution)/shard_map/pallas_call | solution.py:335
  83.5 0.7 copy.13
  84.2 1.1 %copy.14 = f32[12,2,128,128]{3,2,1,0:T(8,128)} copy(f32[12,2,128,128]{3,2,1,0:T(8,128)S(1)} %bitcast.3) | data formatting | bytes 3145728

commit v4 on v3

--- a/solution.py
+++ b/solution.py
@@ -13,6 +13,7 @@
 LANES = 128
 HIT, WRITE = 0, 16
 STRIDE = 5
+UNROLL = 4
 
 
 def nt(a, b, **kw):
@@ -286,7 +287,7 @@
             total = total + jnp.sum(out * out, axis=1, keepdims=True)
         return jnp.where(lane_wide == r, total, sums)
 
-    sums = lax.fori_loop(0, count, carry_in, jnp.zeros((length, LANES), F32))
+    sums = lax.fori_loop(0, count, carry_in, jnp.zeros((length, LANES), F32), unroll=UNROLL)
     flat = jnp.transpose(sums)
     packed = jnp.concatenate([flat[0:8], flat[8:16]], axis=1)
     own_squares[...] = packed
@@ -302,15 +303,11 @@
     inv = lax.rsqrt(total / (width * nz) + 1e-06)
     inv = jnp.transpose(inv)
 
-    def norm(r, carry):
-        low_half = jnp.sum(jnp.where(lane8 == r, inv[0:length], 0.0), axis=1, keepdims=True)
-        high_half = jnp.sum(jnp.where(lane8 == r - 8, inv[length:], 0.0), axis=1, keepdims=True)
-        scale = low_half + high_half
-        attended[r] = (heads[r] * scale * gain[...]).astype(BF16)
-        return carry
-
-    lane8 = lax.broadcasted_iota(jnp.int32, (length, 8), 1)
-    lax.fori_loop(0, count, norm, 0)
+    wide_gain = jnp.broadcast_to(gain[...], (length, width))
+    for r in range(count):
+        down, at = (r // 8) * length, r % 8
+        scale = jnp.broadcast_to(inv[down : down + length, at : at + 1], (length, width))
+        attended[r] = (heads[r] * scale * wide_gain).astype(BF16)
 
     own_new_copy.wait()
     await_all(new_pieces, new_recv, other_pieces)
@@ -321,6 +318,18 @@
     await_all(kv_pieces, kv_send, other_pieces)
     await_all(hit_pieces, hit_send, other_pieces)
     await_all(squares, square_send, nz - 1)
+
+
+def write_out(attended, new_cache, attended_out, new_cache_out, done):
+    quarter = new_cache.shape[0] // 4
+    copies = [pltpu.make_async_copy(attended, attended_out, done.at[4])]
+    for k in range(4):
+        part = pl.ds(k * quarter, quarter)
+        copies.append(pltpu.make_async_copy(new_cache.at[part], new_cache_out.at[part], done.at[k]))
+    for copy in copies:
+        copy.start()
+    for copy in copies:
+        copy.wait()
 
 
 def body(
@@ -384,6 +393,16 @@
             )
         )
     )
+    attended, new_cache = pl.pallas_call(
+        write_out,
+        out_shape=(
+            jax.ShapeDtypeStruct((count, length, width), BF16),
+            jax.ShapeDtypeStruct((entries, tall, size), F32),
+        ),
+        in_specs=[vmem, vmem],
+        out_specs=(pl.BlockSpec(memory_space=pl.ANY),) * 2,
+        scratch_shapes=[sem((5,))],
+    )(*(pltpu.with_memory_space_constraint(a, pltpu.VMEM) for a in (attended, new_cache)))
     return attended, new_cache.reshape(state_cache.shape)
 
 

time: 86.3 us -> 83.5 us (0.968)
  local copies, waits for them, and re-layouts: 1.89 us -> 0 us
    unnamed x2 -> x0, local copies, waits for them, and re-layouts: 1.89 us -> none
    pallas_call x1, Pallas kernels: 82.8 us -> 81.5 us  [body(): pl.pallas_call(functools.partial(kernel, n, nz), out_shape=(pltpu.VMEM((c...]
    pallas_call x0 -> x1, Pallas kernels: none -> 1.31 us  [body(): pl.pallas_call(write_out, out_shape=(jax.ShapeDtypeStruct((count, length,...]
where the time goes in v4:
time: 83.5 us; the launch traced here: 83.4 us
  Pallas kernels  82.8 us (99%)
    pallas_call x1, Pallas kernels, body(): pl.pallas_call(functools.partial(kernel, n, nz), out_shape=(pltpu.VMEM((c...  81.5 us

profile of v4, /device:TPU:1, one launch (start us, length us, event | category | flops | bytes accessed | tf_op | source)
XLA Modules:
  0.0 83.4 jit_solution(15123842350664221139)
XLA Ops:
  0.6 81.5 %shard_map.104 = (bf16[12,64,256]{2,1,0:T(8,128)(2,1)S(1)}, f32[12,256,128]{2,1,0:T(8,128)S(1)}) custom-call(s32[384]{0:T(512)} %slot_hbm.1, s32[12]{0:T(128)} %hit_hbm.1, s32[12]{0:T(128)} %write_hbm.1, f32[12,2,64]{2,1,0:T(2,128)} %log_decay_hbm.1, bf16[12,64,256]{2,1,0:T(8,128)(2,1)} %queries_hbm.1, bf16[12,64,256]{2,1,0:T(8,128)(2,1)} %key_rows_hbm.1, ...), custom_call_target="tpu_custom_call" | custom-call | tf_op jit(solution)/shard_map/pallas_call | solution.py:344
  82.1 1.3 %shard_map.105 = (bf16[12,64,256]{2,1,0:T(8,128)(2,1)}, f32[12,256,128]{2,1,0:T(8,128)}) custom-call(bf16[12,64,256]{2,1,0:T(8,128)(2,1)S(1)} %get-tuple-element.6.attended, f32[12,256,128]{2,1,0:T(8,128)S(1)} %get-tuple-element.7.new_cache), custom_call_target="tpu_custom_call" | custom-call | tf_op jit(solution)/shard_map/pallas_call | solution.py:396

commit v5 on v4

--- a/solution.py
+++ b/solution.py
@@ -13,6 +13,7 @@
 LANES = 128
 HIT, WRITE = 0, 16
 STRIDE = 5
+LATE = 6
 UNROLL = 4
 
 
@@ -31,7 +32,7 @@
     own_decay, decays, source_rows, source_decay, own_squares, squares, log_decay, queries, key_rows, values, gain,
     slots_s, decays_s, source_rows_s, source_decay_s, entry_slot, hit_entry, write_entry,
     slot_send, slot_recv, decay_send, decay_recv, cache_send, cache_recv, kv_send, kv_recv,
-    hit_send, hit_recv, new_send, new_recv, square_send, square_recv, local_sem, plane_in, planes_in,
+    hit_send, hit_recv, new_send, new_recv, square_send, square_recv, local_sem, plane_in, planes_in, first_in,
 ):
     count, length, width = queries.shape
     head_count = log_decay.shape[1]
@@ -99,7 +100,16 @@
     others, other_pieces = n - 1, (n - 1) * count
 
     barrier = pltpu.get_barrier_semaphore()
-    last = n - 1
+    first, last = 0, n - 1
+    waits_late = z == 0
+
+    def each_in_time(act, low=1, high=n):
+        def step(p):
+            @pl.when((p != first) | jnp.logical_not(waits_late))
+            def _():
+                act(p)
+
+        each_peer(step, low, high)
 
     def signal(semaphore, device):
         pl.semaphore_signal(semaphore, inc=1, device_id=device, device_id_type=MESH)
@@ -109,7 +119,11 @@
         def _():
             signal(barrier, (p, z))
 
-    each_peer(greet)
+    @pl.when((me != first) | jnp.logical_not(waits_late))
+    def _():
+        for i in range(1, n):
+            d = i * STRIDE % n
+            greet(lax.rem(x8 + d // 8 * 8, n) + lax.rem(y2 + d // 2 % 4 * 2, 8) + lax.rem(core + d % 2, 2))
 
     def fetch(src, dst, k):
         copy = pltpu.make_async_copy(src, dst, local_sem.at[k])
@@ -130,23 +144,30 @@
     ]
     own_cache_copy = fetch(strip(cache, me), part(pieces, me), 8)
     none = n * count
+
+    @pl.when(me == first)
+    def _():
+        pl.semaphore_wait(barrier, n - 1)
+
+        @pl.when(waits_late)
+        def _():
+            each_peer(lambda p: signal(first_in, (p, z)))
+
+    @pl.when((me != first) & (me != last))
+    def _():
+        pl.semaphore_wait(barrier, n - 1 - jnp.where(waits_late, 1, 0))
+
+    @pl.when(me == last - 1)
+    def _():
+        signal(plane_in, (last, z))
+
+    @pl.when(me == last)
+    def _():
+        pl.semaphore_wait(plane_in, 1)
+
+    each_in_time(lambda p: cache_copy(p).start(), 1, n // 4)
     pieces[pl.ds(none, 8)] = jnp.zeros((8, rows, LANES), F32)
     kv_pieces[pl.ds(none, 8)] = jnp.zeros((8, rows, LANES), F32)
-
-    @pl.when(me != last)
-    def _():
-        pl.semaphore_wait(barrier, n - 1)
-
-    @pl.when(me == last - 1)
-    def _():
-        signal(plane_in, (last, z))
-
-    @pl.when(me == last)
-    def _():
-        pl.semaphore_wait(plane_in, 1)
-        each_z(lambda p: signal(barrier, (me, p)))
-
-    each_peer(lambda p: cache_copy(p).start(), 1, n // 4)
     for copy in tables_in:
         copy.wait()
     lane = lax.broadcasted_iota(jnp.int32, (1, LANES), 1)
@@ -165,9 +186,9 @@
     slots[me] = table
     own_decay[...] = decay_row
     decays[me] = decay_row
-    each_peer(lambda p: slot_copy(p).start())
-    each_peer(lambda p: decay_copy(p).start())
-    each_peer(lambda p: cache_copy(p).start(), n // 4, n)
+    each_in_time(lambda p: slot_copy(p).start())
+    each_in_time(lambda p: decay_copy(p).start())
+    each_in_time(lambda p: cache_copy(p).start(), n // 4, n)
     for copy in rows_in:
         copy.wait()
 
@@ -177,6 +198,13 @@
     lower, upper = jnp.where(causal, 1.0, 0.0), jnp.where(low <= col, 1.0, 0.0)
 
     def block(r, carry):
+        @pl.when(waits_late & (me != first) & (r == LATE + lax.rem(me, count - LATE)))
+        def _():
+            pl.semaphore_wait(first_in, 1)
+            slot_copy(first).start()
+            decay_copy(first).start()
+            cache_copy(first).start()
+
         steps = log_decay[r]
         high = dict(precision=lax.Precision.HIGHEST)
         gsum_rows = jnp.dot(steps, upper, preferred_element_type=F32, **high)
@@ -196,6 +224,11 @@
         return carry
 
     lax.fori_loop(0, count, block, 0)
+
+    @pl.when(me == last)
+    def _():
+        each_z(lambda p: signal(barrier, (me, p)))
+
     own_kv_copy = fetch(strip(kv, me), part(kv_pieces, me), 13)
 
     each_peer(lambda p: kv_copy(p).start())
@@ -378,8 +411,7 @@
             pltpu.SMEM(write_entry.shape, jnp.int32),
             *[sem] * 14,
             sem((16,)),
-            pltpu.SemaphoreType.REGULAR,
-            pltpu.SemaphoreType.REGULAR,
+            *[pltpu.SemaphoreType.REGULAR] * 3,
         ],
         compiler_params=pltpu.CompilerParams(
             collective_id=0, has_side_effects=True, vmem_limit_bytes=32 << 20

time: 83.5 us -> 82.1 us (0.983)
  Pallas kernels: 82.8 us -> 81.4 us
    pallas_call x1, Pallas kernels: 81.5 us -> 80.1 us  [body(): pl.pallas_call(functools.partial(kernel, n, nz), out_shape=(pltpu.VMEM((c...]
where the time goes in v5:
time: 82.1 us; the launch traced here: 82 us
  Pallas kernels  81.4 us (99%)
    pallas_call x1, Pallas kernels, body(): pl.pallas_call(functools.partial(kernel, n, nz), out_shape=(pltpu.VMEM((c...  80.1 us

profile of v5, /device:TPU:1, one launch (start us, length us, event | category | flops | bytes accessed | tf_op | source)
XLA Modules:
  0.0 82.0 jit_solution(14695890342987051083)
XLA Ops:
  0.6 80.1 %shard_map.104 = (bf16[12,64,256]{2,1,0:T(8,128)(2,1)S(1)}, f32[12,256,128]{2,1,0:T(8,128)S(1)}) custom-call(s32[384]{0:T(512)} %slot_hbm.1, s32[12]{0:T(128)} %hit_hbm.1, s32[12]{0:T(128)} %write_hbm.1, f32[12,2,64]{2,1,0:T(2,128)} %log_decay_hbm.1, bf16[12,64,256]{2,1,0:T(8,128)(2,1)} %queries_hbm.1, bf16[12,64,256]{2,1,0:T(8,128)(2,1)} %key_rows_hbm.1, ...), custom_call_target="tpu_custom_call" | custom-call | tf_op jit(solution)/shard_map/pallas_call | solution.py:377
  80.7 1.3 %shard_map.105 = (bf16[12,64,256]{2,1,0:T(8,128)(2,1)}, f32[12,256,128]{2,1,0:T(8,128)}) custom-call(bf16[12,64,256]{2,1,0:T(8,128)(2,1)S(1)} %get-tuple-element.6.attended, f32[12,256,128]{2,1,0:T(8,128)S(1)} %get-tuple-element.7.new_cache), custom_call_target="tpu_custom_call" | custom-call | tf_op jit(solution)/shard_map/pallas_call | solution.py:428

commit v6 on v5

--- a/solution.py
+++ b/solution.py
@@ -114,6 +114,11 @@
     def signal(semaphore, device):
         pl.semaphore_signal(semaphore, inc=1, device_id=device, device_id_type=MESH)
 
+    def each_static(act):
+        for i in range(1, n):
+            d = i * STRIDE % n
+            act(lax.rem(x8 + d // 8 * 8, n) + lax.rem(y2 + d // 2 % 4 * 2, 8) + lax.rem(core + d % 2, 2))
+
     def greet(p):
         @pl.when(p != last)
         def _():
@@ -121,9 +126,7 @@
 
     @pl.when((me != first) | jnp.logical_not(waits_late))
     def _():
-        for i in range(1, n):
-            d = i * STRIDE % n
-            greet(lax.rem(x8 + d // 8 * 8, n) + lax.rem(y2 + d // 2 % 4 * 2, 8) + lax.rem(core + d % 2, 2))
+        each_static(greet)
 
     def fetch(src, dst, k):
         copy = pltpu.make_async_copy(src, dst, local_sem.at[k])
@@ -136,6 +139,30 @@
         fetch(slot_hbm, entry_slot, 2),
         fetch(log_decay_hbm, log_decay, 3),
     ]
+    none = n * count
+
+    @pl.when(me == first)
+    def _():
+        pl.semaphore_wait(barrier, n - 1)
+
+    @pl.when((me != first) & (me != last))
+    def _():
+        pl.semaphore_wait(barrier, n - 1 - jnp.where(waits_late, 1, 0))
+
+    @pl.when(me == last - 1)
+    def _():
+        signal(plane_in, (last, z))
+
+    @pl.when(me == last)
+    def _():
+        pl.semaphore_wait(plane_in, 1)
+
+    each_in_time(lambda p: cache_copy(p).start(), 1, n // 4)
+
+    @pl.when((me == first) & waits_late)
+    def _():
+        each_static(lambda p: signal(first_in, (p, z)))
+
     rows_in = [
         fetch(queries_hbm, queries, 4),
         fetch(key_rows_hbm, key_rows, 5),
@@ -143,29 +170,6 @@
         fetch(gain_hbm, gain, 7),
     ]
     own_cache_copy = fetch(strip(cache, me), part(pieces, me), 8)
-    none = n * count
-
-    @pl.when(me == first)
-    def _():
-        pl.semaphore_wait(barrier, n - 1)
-
-        @pl.when(waits_late)
-        def _():
-            each_peer(lambda p: signal(first_in, (p, z)))
-
-    @pl.when((me != first) & (me != last))
-    def _():
-        pl.semaphore_wait(barrier, n - 1 - jnp.where(waits_late, 1, 0))
-
-    @pl.when(me == last - 1)
-    def _():
-        signal(plane_in, (last, z))
-
-    @pl.when(me == last)
-    def _():
-        pl.semaphore_wait(plane_in, 1)
-
-    each_in_time(lambda p: cache_copy(p).start(), 1, n // 4)
     pieces[pl.ds(none, 8)] = jnp.zeros((8, rows, LANES), F32)
     kv_pieces[pl.ds(none, 8)] = jnp.zeros((8, rows, LANES), F32)
     for copy in tables_in:

time: 82.1 us -> 82.1 us (level)
  no operation moved by 1% of the time
where the time goes in v6:
time: 82.1 us; the launch traced here: 82 us
  Pallas kernels  81.3 us (99%)
    pallas_call x1, Pallas kernels, body(): pl.pallas_call(functools.partial(kernel, n, nz), out_shape=(pltpu.VMEM((c...  80 us

profile of v6, /device:TPU:1, one launch (start us, length us, event | category | flops | bytes accessed | tf_op | source)
XLA Modules:
  0.0 82.0 jit_solution(10518879800595296386)
XLA Ops:
  0.6 80.0 %shard_map.104 = (bf16[12,64,256]{2,1,0:T(8,128)(2,1)S(1)}, f32[12,256,128]{2,1,0:T(8,128)S(1)}) custom-call(s32[384]{0:T(512)} %slot_hbm.1, s32[12]{0:T(128)} %hit_hbm.1, s32[12]{0:T(128)} %write_hbm.1, f32[12,2,64]{2,1,0:T(2,128)} %log_decay_hbm.1, bf16[12,64,256]{2,1,0:T(8,128)(2,1)} %queries_hbm.1, bf16[12,64,256]{2,1,0:T(8,128)(2,1)} %key_rows_hbm.1, ...), custom_call_target="tpu_custom_call" | custom-call | tf_op jit(solution)/shard_map/pallas_call | solution.py:381
  80.7 1.3 %shard_map.105 = (bf16[12,64,256]{2,1,0:T(8,128)(2,1)}, f32[12,256,128]{2,1,0:T(8,128)}) custom-call(bf16[12,64,256]{2,1,0:T(8,128)(2,1)S(1)} %get-tuple-element.6.attended, f32[12,256,128]{2,1,0:T(8,128)S(1)} %get-tuple-element.7.new_cache), custom_call_target="tpu_custom_call" | custom-call | tf_op jit(solution)/shard_map/pallas_call | solution.py:432
